TPU v7x, 256 devices: a whole 4x4x8 slice. The times are simulated.
256 devices in a mesh: expert: 128 (over x, z_hi, y, core), hid: 2 (over z_lo).
Axes of the slice: x: 4, y: 4, z: 8 (z_hi: 4, z_lo: 2; z = z_hi * 2 + z_lo), core: 2. Of those that a mesh axis runs over, the one named last changes fastest.
Arguments:
- tokens: bfloat16 [256, 196, 768], P(('expert', 'hid')), may hold values from -6 to 6
- grad_out: bfloat16 [256, 196, 768], P(('expert', 'hid')), may hold values from -6 to 6
- slot_param: bfloat16 [768, 256], replicated, may hold values from -0.6 to 0.6
- weight_in: bfloat16 [128, 768, 3072], P('expert', None, 'hid'), may hold values from -0.21875 to 0.21875
- weight_out: bfloat16 [128, 3072, 768], P('expert', 'hid'), may hold values from -0.109375 to 0.109375
Outputs:
- grad_tokens: float32 [256, 196, 768], P(('expert', 'hid'))
- grad_weight_in: bfloat16 [128, 768, 3072], P('expert', None, 'hid')
- grad_weight_out: bfloat16 [128, 3072, 768], P('expert', 'hid')
- grad_slot_param: float32 [768, 256], replicated
All inputs are finite; a program needn't handle non-finite values.
Results may differ from a plain program's by a relative error of at most 0.015.
Values may be sent and summed in bfloat16 or wider, within the bound.
A program may use at most 64 MiB of HBM per device.

v0:
```python
import jax
import jax.numpy as jnp
from jax import lax
from jax.sharding import PartitionSpec as P


def gelu_tanh(value):
    return jax.nn.gelu(value, approximate=True)


def take_rows(slot_data):
    sent = lax.all_to_all(slot_data, "expert", split_axis=1, concat_axis=0, tiled=True)
    return lax.all_gather(sent, "hid", axis=0, tiled=True)


def give_back(partial_value):
    summed = lax.psum_scatter(partial_value, "hid", scatter_dimension=0, tiled=True)
    return lax.all_to_all(
        summed.astype(jnp.bfloat16), "expert", split_axis=0, concat_axis=1, tiled=True
    )


def body(tokens, grad_out, slot_param, weight_in, weight_out):
    f32 = jnp.float32
    bf16 = jnp.bfloat16
    model_width = tokens.shape[2]
    expert_local = weight_in.shape[0]
    slot_count = slot_param.shape[1]
    per_slot = slot_count // (expert_local * lax.axis_size("expert"))
    logits = jnp.einsum("bmd,dn->bmn", tokens, slot_param, preferred_element_type=f32)
    dispatch = jax.nn.softmax(logits, axis=1)
    combine = jax.nn.softmax(logits, axis=2)
    dispatch_b = dispatch.astype(bf16)
    combine_b = combine.astype(bf16)
    slot_in = jnp.einsum("bmn,bmd->bnd", dispatch_b, tokens, preferred_element_type=f32).astype(
        bf16
    )
    grad_slot_out = jnp.einsum(
        "bmn,bmd->bnd", combine_b, grad_out, preferred_element_type=f32
    ).astype(bf16)
    gathered = take_rows(slot_in)
    grad_gathered = take_rows(grad_slot_out)
    row_count = gathered.shape[0]
    slot_rows = gathered.reshape(row_count, expert_local, per_slot, model_width)
    pre_act = jnp.einsum("resd,edh->resh", slot_rows, weight_in, preferred_element_type=f32)
    hidden_act = gelu_tanh(pre_act).astype(bf16)
    partial_out = jnp.einsum("resh,ehd->resd", hidden_act, weight_out, preferred_element_type=f32)
    slot_out = give_back(partial_out.reshape(row_count, expert_local * per_slot, model_width))
    grad_combine = jnp.einsum("bmd,bnd->bmn", grad_out, slot_out, preferred_element_type=f32)
    part_combine = (
        combine * (grad_combine - jnp.sum(grad_combine * combine, axis=2, keepdims=True))
    ).astype(bf16)
    grad_rows = grad_gathered.reshape(row_count, expert_local, per_slot, model_width)
    grad_weight_out = jnp.einsum(
        "resh,resd->ehd", hidden_act, grad_rows, preferred_element_type=f32
    ).astype(bf16)
    grad_hidden = jnp.einsum("resd,ehd->resh", grad_rows, weight_out, preferred_element_type=f32)
    grad_pre = jax.vjp(gelu_tanh, pre_act)[1](grad_hidden)[0].astype(bf16)
    grad_weight_in = jnp.einsum(
        "resd,resh->edh", slot_rows, grad_pre, preferred_element_type=f32
    ).astype(bf16)
    partial_in = jnp.einsum("resh,edh->resd", grad_pre, weight_in, preferred_element_type=f32)
    grad_slot_in = give_back(partial_in.reshape(row_count, expert_local * per_slot, model_width))
    grad_dispatch = jnp.einsum("bmd,bnd->bmn", tokens, grad_slot_in, preferred_element_type=f32)
    part_dispatch = (
        dispatch * (grad_dispatch - jnp.sum(grad_dispatch * dispatch, axis=1, keepdims=True))
    ).astype(bf16)
    grad_tokens = jnp.einsum("bmn,bnd->bmd", dispatch_b, grad_slot_in, preferred_element_type=f32)
    grad_tokens = grad_tokens + jnp.einsum(
        "bmn,dn->bmd", part_combine, slot_param, preferred_element_type=f32
    )
    grad_tokens = grad_tokens + jnp.einsum(
        "bmn,dn->bmd", part_dispatch, slot_param, preferred_element_type=f32
    )
    local_grad = jnp.einsum("bmd,bmn->dn", tokens, part_combine, preferred_element_type=f32)
    local_grad = local_grad + jnp.einsum(
        "bmd,bmn->dn", tokens, part_dispatch, preferred_element_type=f32
    )
    grad_slot_param = lax.psum(local_grad, ("expert", "hid"))
    return (grad_tokens, grad_weight_in, grad_weight_out, grad_slot_param)


def solution(mesh):
    return jax.shard_map(
        body,
        mesh=mesh,
        in_specs=(
            P(("expert", "hid"), None, None),
            P(("expert", "hid"), None, None),
            P(),
            P("expert", None, "hid"),
            P("expert", "hid", None),
        ),
        out_specs=(
            P(("expert", "hid"), None, None),
            P("expert", None, "hid"),
            P("expert", "hid", None),
            P(),
        ),
        check_vma=False,
    )
```

profile of v0, /device:TPU:1, one launch (start us, length us, event | category | flops | bytes accessed | tf_op | source)
XLA Modules:
  0.0 468.3 jit_solution(476603769132891541)
XLA Ops:
  7.2 1.6 fusion.42
  9.0 1.3 fusion.21
  10.3 0.6 copy.47
  11.4 3.9 reduce.16
  15.3 1.1 reshape.163
  16.4 34.2 %all_to_all.42 = bf16[128,2,768]{2,1,0:T(2,128)(2,1)} all-to-all(bf16[128,2,768]{2,1,0:T(2,128)(2,1)S(1)} %reshape.163), channel_id=1, replica_groups=mesh['expert'=128,'hid'=2] {'expert'}, dimensions={0} | all-to-all | bytes 786432 | tf_op jit(solution)/shard_map/all_to_all | solution.py:12
  50.6 2.7 reshape.164
  53.3 3.0 bitcast_reduce_fusion.1
  56.3 1.1 all_to_all.15
  57.5 10.0 %all_gather.7 = bf16[256,2,768]{2,0,1:T(8,128)(2,1)S(1)} all-gather(bf16[128,2,768]{2,0,1:T(8,128)(2,1)S(1)} %copy.34), channel_id=1, replica_groups=mesh['expert'=128,'hid'=2] {'hid'}, dimensions={0}, use_global_device_ids=true | all-gather | bytes 1179648 | tf_op jit(solution)/shard_map/all_gather | solution.py:13
  67.5 0.9 copy-done.5
  68.4 3.0 convolution_bitcast_fusion
  71.4 1.7 copy-done.10
  73.1 3.1 fusion.13
  76.9 0.6 copy.48
  77.5 3.9 reduce.17
  81.3 1.1 reshape.165
  82.5 30.2 %all_to_all.43 = bf16[128,2,768]{2,1,0:T(2,128)(2,1)} all-to-all(bf16[128,2,768]{2,1,0:T(2,128)(2,1)S(1)} %reshape.165), channel_id=1, replica_groups=mesh['expert'=128,'hid'=2] {'expert'}, dimensions={0} | all-to-all | bytes 786432 | tf_op jit(solution)/shard_map/all_to_all | solution.py:12
  112.7 2.7 reshape.166
  115.4 3.0 bitcast_reduce_fusion
  118.4 1.1 all_to_all.13
  119.6 10.5 %all_gather.6 = bf16[256,2,768]{2,0,1:T(8,128)(2,1)S(1)} all-gather(bf16[128,2,768]{2,0,1:T(8,128)(2,1)S(1)} %copy.32), channel_id=1, replica_groups=mesh['expert'=128,'hid'=2] {'hid'}, dimensions={0}, use_global_device_ids=true | all-gather | bytes 1179648 | tf_op jit(solution)/shard_map/all_gather | solution.py:13
  130.1 4.8 %fusion.9 = bf16[256,2,1536]{2,0,1:T(8,128)(2,1)S(1)} fusion(f32[256,1,2,1536]{3,0,2,1:T(8,128)} %copy-done.10, bf16[256,2,768]{2,0,1:T(8,128)(2,1)S(1)} %all_gather.6, bf16[1,1536,768]{2,1,0:T(8,128)(2,1)S(1)} %copy-done), kind=kOutput, calls=%fused_computation.16 | convolution fusion | flops 1223688192 | bytes 7864320 | tf_op jit(solution)/shard_map/resd,ehd->resh/dot_general | solution.py:57
  134.9 1.1 copy-done.12
  136.0 2.6 fusion.10
  138.6 1.2 convert_element_type.61
  139.8 1.2 copy.36
  141.0 7.1 %all-to-all-start.3 = ((bf16[128,2,768]{2,1,0:T(2,128)(2,1)}), bf16[128,2,768]{2,1,0:T(2,128)(2,1)S(1)}, u32[]{:S(2)}, u32[]{:S(2)}) async-start(bf16[128,2,768]{2,1,0:T(2,128)(2,1)} %copy.36), calls=%async_computation.5 | async-start | bytes 786432 | tf_op jit(solution)/shard_map/all_to_all | solution.py:18
  148.1 24.9 %reduce-scatter.3.cloned.1.call-done = f32[128,2,768]{2,0,1:T(8,128)} async-done(((f32[256,2,768]{2,0,1:T(8,128)}), f32[128,2,768]{2,0,1:T(8,128)}) %reduce-scatter.3.cloned.1.call-update) | async-done | bytes 786448 | tf_op jit(solution)/shard_map/reduce_scatter | solution.py:17
  172.9 1.2 convert_element_type.59
  174.1 1.2 copy.35
  175.2 13.4 %all-to-all-start.2 = ((bf16[128,2,768]{2,1,0:T(2,128)(2,1)}), bf16[128,2,768]{2,1,0:T(2,128)(2,1)}, u32[]{:S(2)}, u32[]{:S(2)}) async-start(bf16[128,2,768]{2,1,0:T(2,128)(2,1)} %copy.35), calls=%async_computation.3 | async-start | bytes 786432 | tf_op jit(solution)/shard_map/all_to_all | solution.py:18
  188.7 4.6 fusion.7
  193.3 3.2 fusion.8
  196.5 0.9 reshape.156
  197.4 1.4 convolution_bitcast_fusion.3
  198.8 7.0 %all-to-all-done.2 = bf16[128,2,768]{2,1,0:T(2,128)(2,1)} async-done(((bf16[128,2,768]{2,1,0:T(2,128)(2,1)}), bf16[128,2,768]{2,1,0:T(2,128)(2,1)}, u32[]{:S(2)}, u32[]{:S(2)}) %all-to-all-start.2) | async-done | bytes 393248 | tf_op jit(solution)/shard_map/all_to_all | solution.py:18
  205.8 1.1 reshape.154
  206.9 0.7 copy-done.3
  207.7 1.1 fusion.36
  208.8 1.4 multiply_reduce_fusion
  210.7 0.6 copy-done.4
  211.3 1.2 fusion.18
  212.5 1.4 convolution_add_fusion.2
  213.9 1.2 fusion.19
  215.1 1.4 copy.39
  216.5 243.0 %all-reduce.2.cloned.1.call-done = f32[768,256]{0,1:T(8,128)} async-done(((f32[768,256]{0,1:T(8,128)}), f32[768,256]{0,1:T(8,128)}) %all-reduce.2.cloned.1.call-update) | async-done | bytes 786448 | tf_op jit(solution)/shard_map/psum | solution.py:79
  459.5 2.3 copy.40
  (36 shorter events, 2.1 us)
Async XLA Ops:
  7.2 65.9 %copy-start = (bf16[1,1536,768]{2,1,0:T(8,128)(2,1)S(1)}, bf16[1,1536,768]{2,1,0:T(8,128)(2,1)}, u32[]{:S(2)}) copy-start(bf16[1,1536,768]{2,1,0:T(8,128)(2,1)} %param.9) | copy-start | bytes 7077892
  7.2 131.4 %reduce-scatter.5.cloned.1.call-start = ((), (), s32[]{:S(2)}) async-start(), calls=%async_computation.7 | async-start | bytes 2359296 | tf_op jit(solution)/shard_map/reduce_scatter | solution.py:17
  67.5 0.9 copy-start.5
  71.4 1.7 copy-start.10
  73.1 3.4 copy-start.8
  76.2 96.7 %reduce-scatter.3.cloned.1.call-start = ((), (), s32[]{:S(2)}) async-start(), calls=%async_computation.6 | async-start | bytes 2359296 | tf_op jit(solution)/shard_map/reduce_scatter | solution.py:17
  130.1 4.8 %copy-start.6 = (bf16[256,2,768]{2,0,1:T(8,128)(2,1)}, bf16[256,2,768]{2,0,1:T(8,128)(2,1)S(1)}, u32[]{:S(2)}) copy-start(bf16[256,2,768]{2,0,1:T(8,128)(2,1)S(1)} %all_gather.6) | copy-start | bytes 2359300
  130.1 5.9 %copy-start.9 = (bf16[1,768,1536]{2,1,0:T(8,128)(2,1)S(1)}, bf16[1,768,1536]{2,1,0:T(8,128)(2,1)}, u32[]{:S(2)}) copy-start(bf16[1,768,1536]{2,1,0:T(8,128)(2,1)} %param.8) | copy-start | bytes 7077892
  134.9 1.1 copy-start.12
  141.0 34.3 %all-to-all-start.3 = ((bf16[128,2,768]{2,1,0:T(2,128)(2,1)}), bf16[128,2,768]{2,1,0:T(2,128)(2,1)S(1)}, u32[]{:S(2)}, u32[]{:S(2)}) async-start(bf16[128,2,768]{2,1,0:T(2,128)(2,1)} %copy.36), calls=%async_computation.5 | async-start | bytes 786432 | tf_op jit(solution)/shard_map/all_to_all | solution.py:18
  175.2 30.5 %all-to-all-start.2 = ((bf16[128,2,768]{2,1,0:T(2,128)(2,1)}), bf16[128,2,768]{2,1,0:T(2,128)(2,1)}, u32[]{:S(2)}, u32[]{:S(2)}) async-start(bf16[128,2,768]{2,1,0:T(2,128)(2,1)} %copy.35), calls=%async_computation.3 | async-start | bytes 786432 | tf_op jit(solution)/shard_map/all_to_all | solution.py:18
  188.6 270.9 %all-reduce.2.cloned.1.call-start = ((), (), s32[]{:S(2)}) async-start(), calls=%async_computation.8 | async-start | bytes 1572864 | tf_op jit(solution)/shard_map/psum | solution.py:79
  188.7 4.6 copy-start.7
  188.7 4.6 copy-start.11
  196.5 12.2 %copy-start.2 = (bf16[1,196,768]{2,1,0:T(8,128)(2,1)S(1)}, bf16[1,196,768]{2,1,0:T(8,128)(2,1)}, u32[]{:S(2)}) copy-start(bf16[1,196,768]{2,1,0:T(8,128)(2,1)} %param.5) | copy-start | bytes 903172
  206.9 0.7 copy-start.3
  208.7 3.7 copy-start.1
  210.6 0.6 copy-start.4
Sparse Core Ops, SparseCore 0:
  76.3 35.1 reduce-scatter.4
  138.7 34.1 reduce-scatter.2
  212.6 246.8 all-reduce.1
where the time goes:
time: 470 us; the launch traced here: 468 us
  waiting for transfers between devices  275 us (59%)
  blocking collectives  84.8 us (18%)
  matrix products  32.6 us (7%)
  local copies, waits for them, and re-layouts  30.9 us (7%)
  starting transfers between devices  20.8 us (4%)
  between operations  14 us (3%)
  other arithmetic  10.3 us (2%)
    psum x1, waiting for transfers between devices, body(): grad_slot_param = lax.psum(local_grad, ('expert', 'hid'))  243 us
    all_to_all x2, blocking collectives, take_rows(): lax.all_to_all(slot_data, 'expert', split_axis=1, concat_axis=0, tiled=True)  64.4 us
    reduce_scatter x2, waiting for transfers between devices, give_back(): lax.psum_scatter(partial_value, 'hid', scatter_dimension=0, tiled=True)  24.9 us
    all_to_all x2, starting transfers between devices, give_back(): lax.all_to_all(summed.astype(jnp.bfloat16), 'expert', split_axis=0, conca...  20.5 us
    all_gather x2, blocking collectives, take_rows(): return lax.all_gather(sent, 'hid', axis=0, tiled=True)  20.5 us
    unnamed x33, local copies, waits for them, and re-layouts  17 us
  transfers between devices with their start and end apart: 5, of which 3 were waited for; matrix products, arithmetic and copies ran while one was open for 8% of the time, Pallas kernels for 0%

commit v1 on v0

v1 whole, which is shorter than its diff:
```python
import math

import jax
import jax.numpy as jnp
from jax import lax
from jax.experimental import pallas as pl
from jax.experimental.pallas import tpu as pltpu
from jax.sharding import PartitionSpec as P

F32 = jnp.float32
BF16 = jnp.bfloat16
MESH = pl.DeviceIdType.MESH

TOKENS = 196
PAD = 208
WIDTH = 768
HALF_HIDDEN = 1536
SLOTS = 256
ROWS = 512
NEAR = 256
BLOCK = 32
TILE = 256
ROOT = math.sqrt(2.0 / math.pi)


def dot(left, right, left_dim=1, right_dim=0):
    return lax.dot_general(
        left, right, (((left_dim,), (right_dim,)), ((), ())), preferred_element_type=F32
    )


def one_hot(rows, columns, source):
    row = lax.broadcasted_iota(jnp.int32, (rows, columns), 0)
    column = lax.broadcasted_iota(jnp.int32, (rows, columns), 1)
    return jnp.where(source(row) == column, 1.0, 0.0).astype(BF16)


def swap_slots(index):
    return (index & 0xC3) | ((index & 0x30) >> 2) | ((index & 0x0C) << 2)


def to_line(index):
    return (((index >> 1) & 15) << 4) | ((index >> 5) << 1) | (index & 1)


def to_plane(index):
    return (((index >> 1) & 7) << 5) | ((index >> 4) << 1) | (index & 1)


def kernel(
    tok_ref,
    go_ref,
    sp_ref,
    win_hbm,
    wout_hbm,
    gt_ref,
    gwi_hbm,
    gwo_hbm,
    gsp_ref,
    tok,
    go,
    tok_t,
    spp,
    disp,
    comb,
    disp_b,
    win,
    wout,
    plane_out,
    plane_in,
    line_out,
    line_in,
    rows,
    twin_out,
    twin_in,
    own,
    act,
    slope,
    gpre,
    gwi,
    gwo,
    acc_t,
    grad,
    grad_core,
    ar_out,
    ar_in,
    z_out,
    z_in,
    done,
    w_sem,
    o_sem,
    p_send,
    p_recv,
    l_send,
    l_recv,
    f_send,
    f_recv,
    c_send,
    c_recv,
    a_send,
    a_recv,
    g_send,
    g_recv,
    z_send,
    z_recv,
):
    expert = lax.axis_index("expert")
    zl = lax.axis_index("hid")
    x = expert >> 5
    zh = (expert >> 3) & 3
    y = (expert >> 1) & 3
    c = expert & 1
    z = zh * 2 + zl
    mine = x * 4 + y
    side = 2 * zl - 1

    def device(px, py, pz, pc):
        return {
            "expert": (((px * 4 + (pz >> 1)) * 4 + py) * 2) + pc,
            "hid": pz & 1,
        }

    twin = device(x, y, z ^ 1, c)
    sibling = device(x, y, z, c ^ 1)

    def plane_peer(k):
        return (x + (k >> 2)) & 3, (y + (k & 3)) & 3

    w_copies = [
        pltpu.make_async_copy(win_hbm.at[0], win, w_sem.at[0]),
        pltpu.make_async_copy(wout_hbm.at[0], wout, w_sem.at[1]),
    ]
    for copy in w_copies:
        copy.start()

    barrier = pltpu.get_barrier_semaphore()

    @pl.loop(1, 16)
    def _(k):
        px, py = plane_peer(k)
        pl.semaphore_signal(barrier, inc=1, device_id=device(px, py, z, c), device_id_type=MESH)
        pl.semaphore_signal(
            barrier,
            inc=1,
            device_id=device(x, y, (z + (k >> 1)) & 7, c ^ (k & 1)),
            device_id_type=MESH,
        )

    def block16(index):
        return pl.ds(pl.multiple_of(index * 16, 16), 16)

    def block32(index):
        return pl.ds(pl.multiple_of(index * BLOCK, BLOCK), BLOCK)

    def plane_copy(a, k):
        px, py = plane_peer(k)
        return pltpu.make_async_remote_copy(
            src_ref=plane_out.at[a, block16(px * 4 + py)],
            dst_ref=plane_in.at[a, block16(mine)],
            send_sem=p_send.at[a, k],
            recv_sem=p_recv.at[a, k],
            device_id=device(px, py, z, c),
            device_id_type=MESH,
        )

    def plane_start(a):
        @pl.loop(1, 16)
        def _(k):
            plane_copy(a, k).start()

        plane_in[a, block16(mine)] = plane_out[a, block16(mine)]

    def plane_finish(a):
        @pl.loop(1, 16)
        def _(k):
            plane_copy(a, k).wait_recv()

    def line_copy(a, j):
        q = (zh + (j >> 1)) & 3
        pc = c ^ (j & 1)
        k = (z - 2 * q + 11) & 7
        low = k >> 2
        far = jnp.where(low == 1, k - 4, 3 - k)
        return pltpu.make_async_remote_copy(
            src_ref=line_out.at[a, block32(q * 2 + pc)],
            dst_ref=rows.at[a, block32(k * 2 + c)],
            send_sem=l_send.at[a, j],
            recv_sem=l_recv.at[a, far * 2 + (j & 1)],
            device_id=device(x, y, 2 * q + low, pc),
            device_id_type=MESH,
        )

    def near_row(t, pc):
        return (3 + zl + side * t) * 2 + pc

    def line_start(a):
        @pl.loop(1, 8)
        def _(j):
            line_copy(a, j).start()

        rows[a, block32((3 + zl) * 2 + c)] = line_out[a, block32(zh * 2 + c)]

    def arrive(a, j):
        place = block32(near_row(j >> 1, c ^ (j & 1)))
        return pltpu.make_async_remote_copy(
            src_ref=rows.at[a, place],
            dst_ref=rows.at[a, place],
            send_sem=f_send.at[a, j],
            recv_sem=l_recv.at[a, j],
            device_id=twin,
            device_id_type=MESH,
        )

    def forward(a, j):
        place = block32(near_row(j >> 1, c ^ (j & 1)))
        return pltpu.make_async_remote_copy(
            src_ref=rows.at[a, place],
            dst_ref=rows.at[a, place],
            send_sem=f_send.at[a, j],
            recv_sem=f_recv.at[a, j],
            device_id=twin,
            device_id_type=MESH,
        )

    def pass_on(a):
        forward(a, 0).start()

        @pl.loop(1, 8)
        def _(j):
            arrive(a, j).wait_recv()
            forward(a, j).start()

    def far_finish(a):
        @pl.loop(0, 8)
        def _(j):
            forward(a, j).wait_recv()

    def twin_copy(a, t):
        place = pl.ds(pl.multiple_of(t * 64, 64), 64)
        return pltpu.make_async_remote_copy(
            src_ref=twin_out.at[a, place],
            dst_ref=twin_in.at[a, place],
            send_sem=c_send.at[a, t],
            recv_sem=c_recv.at[a, t],
            device_id=twin,
            device_id_type=MESH,
        )

    def back_copy(a, j):
        t = j >> 1
        pc = c ^ (j & 1)
        pz = (z + side * t + 8) & 7
        shift = (zh - (pz >> 1) + 4) & 3
        return pltpu.make_async_remote_copy(
            src_ref=line_out.at[2 + a, block32(near_row(t, pc) - 8 * zl)],
            dst_ref=line_in.at[a, block32(zh * 2 + c)],
            send_sem=l_send.at[2 + a, j],
            recv_sem=l_recv.at[2 + a, shift * 2 + (j & 1)],
            device_id=device(x, y, pz, pc),
            device_id_type=MESH,
        )

    near_rows = pl.ds(pl.multiple_of(zl * NEAR, NEAR), NEAR)
    far_rows = pl.ds(pl.multiple_of((1 - zl) * NEAR, NEAR), NEAR)

    def back_finish(a):
        @pl.loop(1, 8)
        def _(j):
            pltpu.make_async_remote_copy(
                src_ref=line_in.at[a, block32(0)],
                dst_ref=line_in.at[a, block32(0)],
                send_sem=l_send.at[2 + a, j],
                recv_sem=l_recv.at[2 + a, j],
                device_id=twin,
                device_id_type=MESH,
            ).wait_recv()

    tok[...] = jnp.zeros_like(tok)
    tok[0:TOKENS, :] = tok_ref[0]
    go[...] = jnp.zeros_like(go)
    go[0:TOKENS, :] = go_ref[0]
    swap = one_hot(SLOTS, SLOTS, swap_slots)
    spp[...] = dot(sp_ref[...], swap).astype(BF16)
    logits = dot(tok[...], spp[...])
    valid = lax.broadcasted_iota(jnp.int32, (PAD, SLOTS), 0) < TOKENS
    masked = jnp.where(valid, logits, -1e30)
    raised = jnp.exp(masked - jnp.max(masked, axis=0, keepdims=True))
    dispatch = raised / jnp.sum(raised, axis=0, keepdims=True)
    disp[...] = dispatch
    disp_b[...] = dispatch.astype(BF16)
    plane_out[0] = dot(disp_b[...], tok[...], 0, 0).astype(BF16)
    pl.semaphore_wait(barrier, 30)
    plane_start(0)
    raised = jnp.exp(logits - jnp.max(logits, axis=1, keepdims=True))
    combine = raised / jnp.sum(raised, axis=1, keepdims=True)
    comb[...] = combine
    plane_out[1] = dot(combine.astype(BF16), go[...], 0, 0).astype(BF16)
    plane_start(1)
    tok_t[...] = tok[...].T

    line = one_hot(SLOTS, SLOTS, to_line)
    for a in range(2):
        plane_finish(a)
        line_out[a] = dot(line, plane_in[a]).astype(BF16)
        line_start(a)
    pass_on(0)
    for copy in w_copies:
        copy.wait()
    far_finish(0)

    @pl.loop(0, HALF_HIDDEN // TILE)
    def _(j):
        tile = pl.ds(pl.multiple_of(j * TILE, TILE), TILE)
        pre = dot(rows[0], win[:, tile])
        square = pre * pre
        tanh = jnp.tanh(ROOT * pre * (1.0 + 0.044715 * square))
        half = 0.5 * (1.0 + tanh)
        act[:, tile] = (pre * half).astype(BF16)
        slope[:, tile] = half + (0.5 * ROOT) * pre * (1.0 - tanh * tanh) * (
            1.0 + (3 * 0.044715) * square
        )

    def send_back(a, wide, weight, weight_dim):
        def piece(place, j):
            tile = pl.ds(pl.multiple_of(j * TILE, TILE), TILE)
            if weight_dim == 0:
                return tile, dot(wide[place], weight[:, tile])
            return tile, dot(wide[place], weight[tile, :], 1, 1)

        @pl.loop(0, WIDTH // TILE)
        def _(j):
            tile, value = piece(far_rows, j)
            twin_out[a, :, tile] = value.astype(BF16)

        @pl.loop(0, 4)
        def _(t):
            twin_copy(a, t).start()

        @pl.loop(0, WIDTH // TILE)
        def _(j):
            tile, value = piece(near_rows, j)
            own[:, tile] = value

    def sum_back(a):
        @pl.loop(0, 4)
        def _(t):
            twin_copy(a, t).wait_recv()

        line_out[2 + a] = (own[...] + twin_in[a].astype(F32)).astype(BF16)

        @pl.loop(1, 8)
        def _(j):
            back_copy(a, j).start()

        line_in[a, block32(zh * 2 + c)] = line_out[2 + a, block32(near_row(0, c) - 8 * zl)]

    send_back(0, act, wout, 0)
    pass_on(1)
    sum_back(0)
    far_finish(1)

    @pl.loop(0, HALF_HIDDEN // TILE)
    def _(j):
        tile = pl.ds(pl.multiple_of(j * TILE, TILE), TILE)
        gpre[:, tile] = (dot(rows[1], wout[tile, :], 1, 1) * slope[:, tile]).astype(BF16)

    send_back(1, gpre, win, 1)
    plane = one_hot(SLOTS, SLOTS, to_plane)
    back_finish(0)
    plane_out[2] = dot(plane, line_in[0]).astype(BF16)
    plane_start(2)
    sum_back(1)

    def out_copies(j):
        tile = pl.ds(pl.multiple_of(j * TILE, TILE), TILE)
        return pltpu.make_async_copy(gwo.at[tile], gwo_hbm.at[0, tile], o_sem.at[0, j])

    def in_copies(j):
        tile = pl.ds(pl.multiple_of(j * TILE, TILE), TILE)
        return pltpu.make_async_copy(gwi.at[tile], gwi_hbm.at[0, tile], o_sem.at[1, j])

    @pl.loop(0, HALF_HIDDEN // TILE)
    def _(j):
        tile = pl.ds(pl.multiple_of(j * TILE, TILE), TILE)
        gwo[tile, :] = dot(act[:, tile], rows[1], 0, 0).astype(BF16)
        out_copies(j).start()

    @pl.loop(0, WIDTH // TILE)
    def _(j):
        tile = pl.ds(pl.multiple_of(j * TILE, TILE), TILE)
        gwi[tile, :] = dot(rows[0, :, tile], gpre[...], 0, 0).astype(BF16)
        in_copies(j).start()

    back_finish(1)
    plane_out[3] = dot(plane, line_in[1]).astype(BF16)
    plane_start(3)
    plane_finish(2)
    gc = dot(go[...], plane_in[2], 1, 1)
    weight = comb[...]
    part = dot(
        (weight * (gc - jnp.sum(gc * weight, axis=1, keepdims=True))).astype(BF16), swap
    ).astype(BF16)
    acc_t[...] = dot(part, sp_ref[...], 1, 1)
    grad_half = dot(tok_t[...], part)
    grad[0] = grad_half[:, 0:128]
    grad[1] = grad_half[:, 128:256]
    plane_finish(3)
    gd = dot(tok[...], plane_in[3], 1, 1)
    weight = disp[...]
    part = dot(
        (weight * (gd - jnp.sum(gd * weight, axis=0, keepdims=True))).astype(BF16), swap
    ).astype(BF16)
    grad_half = dot(tok_t[...], part)
    grad[0] += grad_half[:, 0:128]
    grad[1] += grad_half[:, 128:256]

    core_copy = pltpu.make_async_remote_copy(
        src_ref=grad.at[c ^ 1],
        dst_ref=grad_core,
        send_sem=g_send.at[0],
        recv_sem=g_recv.at[0],
        device_id=sibling,
        device_id_type=MESH,
    )
    core_copy.start()
    total = acc_t[...] + dot(part, sp_ref[...], 1, 1) + dot(disp_b[...], plane_in[3])
    gt_ref[0] = total[0:TOKENS]
    core_copy.wait_recv()
    ar_out[...] = (grad[c] + grad_core[...]).astype(BF16)

    def block48(index):
        return pl.ds(pl.multiple_of(index * 48, 48), 48)

    def reduce_copy(k):
        px, py = plane_peer(k)
        return pltpu.make_async_remote_copy(
            src_ref=ar_out.at[block48(px * 4 + py)],
            dst_ref=ar_in.at[block48(mine)],
            send_sem=a_send.at[0, k],
            recv_sem=a_recv.at[0, k],
            device_id=device(px, py, z, c),
            device_id_type=MESH,
        )

    @pl.loop(1, 16)
    def _(k):
        reduce_copy(k).start()

    ar_in[block48(mine)] = ar_out[block48(mine)]

    @pl.loop(1, 16)
    def _(k):
        reduce_copy(k).wait_recv()

    plane_sum = ar_in[0:48].astype(F32)
    for k in range(1, 16):
        plane_sum += ar_in[48 * k : 48 * k + 48].astype(F32)
    z_out[...] = plane_sum.astype(BF16)

    def z_copy(k):
        return pltpu.make_async_remote_copy(
            src_ref=z_out,
            dst_ref=z_in.at[z],
            send_sem=z_send.at[k],
            recv_sem=z_recv.at[k],
            device_id=device(x, y, (z + k) & 7, c),
            device_id_type=MESH,
        )

    @pl.loop(1, 8)
    def _(k):
        z_copy(k).start()

    z_in[z] = z_out[...]

    @pl.loop(1, 8)
    def _(k):
        z_copy(k).wait_recv()

    line_sum = z_in[0].astype(F32)
    for k in range(1, 8):
        line_sum += z_in[k].astype(F32)
    done[c, block48(mine)] = line_sum

    def gather_copy(k):
        px, py = plane_peer(k)
        return pltpu.make_async_remote_copy(
            src_ref=done.at[c, block48(mine)],
            dst_ref=done.at[c, block48(mine)],
            send_sem=a_send.at[1, k],
            recv_sem=a_recv.at[1, k],
            device_id=device(px, py, z, c),
            device_id_type=MESH,
        )

    @pl.loop(1, 16)
    def _(k):
        gather_copy(k).start()

    @pl.loop(1, 16)
    def _(k):
        gather_copy(k).wait_recv()

    last_copy = pltpu.make_async_remote_copy(
        src_ref=done.at[c],
        dst_ref=done.at[c],
        send_sem=g_send.at[1],
        recv_sem=g_recv.at[1],
        device_id=sibling,
        device_id_type=MESH,
    )
    last_copy.start()

    @pl.loop(1, 16)
    def _(k):
        for a in range(4):
            plane_copy(a, k).wait_send()
        reduce_copy(k).wait_send()
        gather_copy(k).wait_send()

    @pl.loop(1, 8)
    def _(k):
        z_copy(k).wait_send()
        for a in range(2):
            line_copy(a, k).wait_send()
            back_copy(a, k).wait_send()

    @pl.loop(0, 8)
    def _(k):
        for a in range(2):
            forward(a, k).wait_send()

    @pl.loop(0, 4)
    def _(t):
        for a in range(2):
            twin_copy(a, t).wait_send()

    core_copy.wait_send()

    @pl.loop(0, HALF_HIDDEN // TILE)
    def _(j):
        out_copies(j).wait()

    @pl.loop(0, WIDTH // TILE)
    def _(j):
        in_copies(j).wait()

    last_copy.wait()
    gsp_ref[:, 0:128] = done[0]
    gsp_ref[:, 128:256] = done[1]


def body(tokens, grad_out, slot_param, weight_in, weight_out):
    vmem = pl.BlockSpec(memory_space=pltpu.VMEM)
    hbm = pl.BlockSpec(memory_space=pl.ANY)
    dma = pltpu.SemaphoreType.DMA
    buffers = [
        ((PAD, WIDTH), BF16),
        ((PAD, WIDTH), BF16),
        ((WIDTH, PAD), BF16),
        ((WIDTH, SLOTS), BF16),
        ((PAD, SLOTS), F32),
        ((PAD, SLOTS), F32),
        ((PAD, SLOTS), BF16),
        ((WIDTH, HALF_HIDDEN), BF16),
        ((HALF_HIDDEN, WIDTH), BF16),
        ((4, SLOTS, WIDTH), BF16),
        ((4, SLOTS, WIDTH), BF16),
        ((4, SLOTS, WIDTH), BF16),
        ((2, SLOTS, WIDTH), BF16),
        ((2, ROWS, WIDTH), BF16),
        ((2, NEAR, WIDTH), BF16),
        ((2, NEAR, WIDTH), BF16),
        ((NEAR, WIDTH), F32),
        ((ROWS, HALF_HIDDEN), BF16),
        ((ROWS, HALF_HIDDEN), F32),
        ((ROWS, HALF_HIDDEN), BF16),
        ((WIDTH, HALF_HIDDEN), BF16),
        ((HALF_HIDDEN, WIDTH), BF16),
        ((PAD, WIDTH), F32),
        ((2, WIDTH, 128), F32),
        ((WIDTH, 128), F32),
        ((WIDTH, 128), BF16),
        ((WIDTH, 128), BF16),
        ((48, 128), BF16),
        ((8, 48, 128), BF16),
        ((2, WIDTH, 128), F32),
    ]
    return pl.pallas_call(
        kernel,
        out_shape=(
            jax.ShapeDtypeStruct(tokens.shape, F32),
            jax.ShapeDtypeStruct(weight_in.shape, BF16),
            jax.ShapeDtypeStruct(weight_out.shape, BF16),
            jax.ShapeDtypeStruct(slot_param.shape, F32),
        ),
        in_specs=[vmem, vmem, vmem, hbm, hbm],
        out_specs=(vmem, hbm, hbm, vmem),
        scratch_shapes=[pltpu.VMEM(shape, kind) for shape, kind in buffers]
        + [
            dma((2,)),
            dma((2, 8)),
            dma((4, 16)),
            dma((4, 16)),
            dma((4, 8)),
            dma((4, 8)),
            dma((2, 8)),
            dma((2, 8)),
            dma((2, 4)),
            dma((2, 4)),
            dma((2, 16)),
            dma((2, 16)),
            dma((2,)),
            dma((2,)),
            dma((8,)),
            dma((8,)),
        ],
        compiler_params=pltpu.CompilerParams(
            collective_id=0, has_side_effects=True, vmem_limit_bytes=56 * 1024 * 1024
        ),
    )(tokens, grad_out, slot_param, weight_in, weight_out)


def solution(mesh):
    return jax.shard_map(
        body,
        mesh=mesh,
        in_specs=(
            P(("expert", "hid"), None, None),
            P(("expert", "hid"), None, None),
            P(),
            P("expert", None, "hid"),
            P("expert", "hid", None),
        ),
        out_specs=(
            P(("expert", "hid"), None, None),
            P("expert", None, "hid"),
            P("expert", "hid", None),
            P(),
        ),
        check_vma=False,
    )
```

time: 470 us -> 137 us (0.29)
  waiting for transfers between devices: 275 us -> 0 us
  Pallas kernels: 0 us -> 127 us
  blocking collectives: 84.8 us -> 0 us
  matrix products: 32.6 us -> 0 us
  local copies, waits for them, and re-layouts: 30.9 us -> 8.44 us
  starting transfers between devices: 20.8 us -> 0 us
  between operations: 14 us -> 0.64 us
  other arithmetic: 10.3 us -> 0 us
    psum x1 -> x0, waiting for transfers between devices: 243 us -> none  [body(): grad_slot_param = lax.psum(local_grad, ('expert', 'hid'))]
    pallas_call x0 -> x1, Pallas kernels: none -> 127 us  [body(): pl.pallas_call(kernel, out_shape=(jax.ShapeDtypeStruct(tokens.shape, F32)...]
    all_to_all x2 -> x0, blocking collectives: 64.4 us -> none  [take_rows(): lax.all_to_all(slot_data, 'expert', split_axis=1, concat_axis=0, tiled=True)]
    dot_general x16 -> x0, matrix products: 32.6 us -> none  [the longest x1 4.76 us: body(): jnp.einsum('resd,ehd->resh', grad_rows, weight_out, preferred_element_typ...]
    reduce_scatter x2 -> x0, waiting for transfers between devices: 24.9 us -> none  [give_back(): lax.psum_scatter(partial_value, 'hid', scatter_dimension=0, tiled=True)]
    all_to_all x2 -> x0, starting transfers between devices: 20.5 us -> none  [give_back(): lax.all_to_all(summed.astype(jnp.bfloat16), 'expert', split_axis=0, conca...]
    all_gather x2 -> x0, blocking collectives: 20.5 us -> none  [take_rows(): return lax.all_gather(sent, 'hid', axis=0, tiled=True)]
    unnamed x33 -> x7, local copies, waits for them, and re-layouts: 17 us -> 5.93 us
  transfers between devices with their start and end apart: 5 -> 0, of which waited for: 3 -> 0; matrix products, arithmetic and copies ran while one was open for 8% -> 0% of each run, Pallas kernels for 0% -> 0%
where the time goes in v1:
time: 137 us; the launch traced here: 136 us
  Pallas kernels  127 us (93%)
  local copies, waits for them, and re-layouts  8.44 us (6%)
    pallas_call x1, Pallas kernels, body(): pl.pallas_call(kernel, out_shape=(jax.ShapeDtypeStruct(tokens.shape, F32)...  127 us
    unnamed x7, local copies, waits for them, and re-layouts  5.93 us

profile of v1, /device:TPU:1, one launch (start us, length us, event | category | flops | bytes accessed | tf_op | source)
XLA Modules:
  0.0 136.3 jit_solution(12333063058276072797)
XLA Ops:
  0.6 127.2 %shard_map.84 = (f32[1,196,768]{2,1,0:T(8,128)}, bf16[1,768,1536]{2,1,0:T(8,128)(2,1)}, bf16[1,1536,768]{2,1,0:T(8,128)(2,1)}, f32[768,256]{1,0:T(8,128)}) custom-call(bf16[1,196,768]{2,1,0:T(8,128)(2,1)} %tok_ref.1, bf16[1,196,768]{2,1,0:T(8,128)(2,1)} %go_ref.1, bf16[768,256]{1,0:T(8,128)(2,1)} %sp_ref.1, bf16[1,768,1536]{2,1,0:T(8,128)(2,1)} %win_hbm.1, ...), custom_call_target="tpu_custom_call" | custom-call | tf_op jit(solution)/shard_map/pallas_call | solution.py:589
  127.9 2.5 %copy.9 = f32[1,196,768]{2,0,1:T(1,128)} copy(f32[1,196,768]{2,1,0:T(8,128)} %get-tuple-element.4) | data formatting | bytes 1204224 | tf_op jit(solution)/shard_map/pallas_call | solution.py:589
  130.4 0.0 copy-start
  130.4 3.4 %copy.13 = bf16[1,768,1536]{2,1,0:T(8,128)(2,1)} copy(bf16[1,768,1536]{2,1,0:T(8,128)(2,1)} %get-tuple-element.13) | data formatting | bytes 4718592
  133.8 0.0 copy-done
  133.8 0.0 copy-start.1
  133.8 1.4 %copy.14 = bf16[1,1536,768]{2,1,0:T(8,128)(2,1)} copy(bf16[1,1536,768]{2,1,0:T(8,128)(2,1)S(1)} %copy-done) | data formatting | bytes 4718592
  135.2 0.3 copy-done.1
  135.4 0.9 copy.15
Async XLA Ops:
  130.4 3.4 %copy-start = (bf16[1,1536,768]{2,1,0:T(8,128)(2,1)S(1)}, bf16[1,1536,768]{2,1,0:T(8,128)(2,1)}, u32[]{:S(2)}) copy-start(bf16[1,1536,768]{2,1,0:T(8,128)(2,1)} %get-tuple-element.14) | copy-start | bytes 7077892
  133.8 1.7 %copy-start.1 = (f32[768,256]{1,0:T(8,128)S(1)}, f32[768,256]{1,0:T(8,128)}, u32[]{:S(2)}) copy-start(f32[768,256]{1,0:T(8,128)} %get-tuple-element.15) | copy-start | bytes 2359300

commit v2 on v1

--- a/solution.py
+++ b/solution.py
@@ -19,6 +19,7 @@
 ROWS = 512
 NEAR = 256
 BLOCK = 32
+HALF = 384
 TILE = 256
 ROOT = math.sqrt(2.0 / math.pi)
 
@@ -48,15 +49,24 @@
 
 
 def kernel(
+    tok_hbm,
+    go_hbm,
+    sp_hbm,
+    win_hbm,
+    wout_hbm,
+    gt_hbm,
+    gwi_hbm,
+    gwo_hbm,
+    gsp_hbm,
     tok_ref,
     go_ref,
     sp_ref,
-    win_hbm,
-    wout_hbm,
-    gt_ref,
-    gwi_hbm,
-    gwo_hbm,
-    gsp_ref,
+    line,
+    plane,
+    swap,
+    part_s,
+    gt,
+    gsp,
     tok,
     go,
     tok_t,
@@ -81,7 +91,8 @@
     gwo,
     acc_t,
     grad,
-    grad_core,
+    core_out,
+    core_in,
     ar_out,
     ar_in,
     z_out,
@@ -126,11 +137,16 @@
     def plane_peer(k):
         return (x + (k >> 2)) & 3, (y + (k & 3)) & 3
 
+    i_copies = [
+        pltpu.make_async_copy(sp_hbm, sp_ref, w_sem.at[2]),
+        pltpu.make_async_copy(tok_hbm, tok_ref, w_sem.at[3]),
+        pltpu.make_async_copy(go_hbm, go_ref, w_sem.at[4]),
+    ]
     w_copies = [
         pltpu.make_async_copy(win_hbm.at[0], win, w_sem.at[0]),
         pltpu.make_async_copy(wout_hbm.at[0], wout, w_sem.at[1]),
     ]
-    for copy in w_copies:
+    for copy in i_copies + w_copies:
         copy.start()
 
     barrier = pltpu.get_barrier_semaphore()
@@ -163,6 +179,31 @@
             device_id_type=MESH,
         )
 
+    def half_copy(h, k):
+        px, py = plane_peer(k)
+        columns = pl.ds(h * HALF, HALF)
+        return pltpu.make_async_remote_copy(
+            src_ref=plane_out.at[0, block16(px * 4 + py), columns],
+            dst_ref=plane_in.at[0, block16(mine), columns],
+            send_sem=p_send.at[4 * h, k],
+            recv_sem=p_recv.at[4 * h, k],
+            device_id=device(px, py, z, c),
+            device_id_type=MESH,
+        )
+
+    def half_start(h):
+        @pl.loop(1, 16)
+        def _(k):
+            half_copy(h, k).start()
+
+        columns = pl.ds(h * HALF, HALF)
+        plane_in[0, block16(mine), columns] = plane_out[0, block16(mine), columns]
+
+    def half_finish(h):
+        @pl.loop(1, 16)
+        def _(k):
+            half_copy(h, k).wait_recv()
+
     def plane_start(a):
         @pl.loop(1, 16)
         def _(k):
@@ -175,15 +216,15 @@
         def _(k):
             plane_copy(a, k).wait_recv()
 
-    def line_copy(a, j):
+    def line_copy(a, j, columns=pl.ds(0, WIDTH)):
         q = (zh + (j >> 1)) & 3
         pc = c ^ (j & 1)
         k = (z - 2 * q + 11) & 7
         low = k >> 2
         far = jnp.where(low == 1, k - 4, 3 - k)
         return pltpu.make_async_remote_copy(
-            src_ref=line_out.at[a, block32(q * 2 + pc)],
-            dst_ref=rows.at[a, block32(k * 2 + c)],
+            src_ref=line_out.at[a, block32(q * 2 + pc), columns],
+            dst_ref=rows.at[a, block32(k * 2 + c), columns],
             send_sem=l_send.at[a, j],
             recv_sem=l_recv.at[a, far * 2 + (j & 1)],
             device_id=device(x, y, 2 * q + low, pc),
@@ -193,12 +234,27 @@
     def near_row(t, pc):
         return (3 + zl + side * t) * 2 + pc
 
-    def line_start(a):
-        @pl.loop(1, 8)
-        def _(j):
-            line_copy(a, j).start()
-
-        rows[a, block32((3 + zl) * 2 + c)] = line_out[a, block32(zh * 2 + c)]
+    def own_copy(a, j, columns):
+        pc = c ^ j
+        return pltpu.make_async_remote_copy(
+            src_ref=line_out.at[a, block32(zh * 2 + pc), columns],
+            dst_ref=rows.at[a, block32((3 + zl) * 2 + c), columns],
+            send_sem=f_send.at[a, j],
+            recv_sem=f_recv.at[a, j],
+            device_id=device(x, y, z ^ 1, pc),
+            device_id_type=MESH,
+        )
+
+    def line_start(a, columns=pl.ds(0, WIDTH)):
+        for dq in (1, 3):
+            for dc in range(2):
+                line_copy(a, 2 * dq + dc, columns).start()
+        line_copy(a, 1, columns).start()
+        for dc in range(2):
+            own_copy(a, dc, columns).start()
+        for dc in range(2):
+            line_copy(a, 4 + dc, columns).start()
+        rows[a, block32((3 + zl) * 2 + c), columns] = line_out[a, block32(zh * 2 + c), columns]
 
     def arrive(a, j):
         place = block32(near_row(j >> 1, c ^ (j & 1)))
@@ -222,21 +278,25 @@
             device_id_type=MESH,
         )
 
-    def pass_on(a):
-        forward(a, 0).start()
-
-        @pl.loop(1, 8)
-        def _(j):
+    def pass_on(a, t):
+        for dc in range(2):
+            j = 2 * t + dc
             arrive(a, j).wait_recv()
             forward(a, j).start()
+
+    def own_finish(a):
+        arrive(a, 1).wait_recv()
 
     def far_finish(a):
         @pl.loop(0, 8)
         def _(j):
             forward(a, j).wait_recv()
 
+    def near_chunk(low, t):
+        return 3 - 3 * low + (2 * low - 1) * t
+
     def twin_copy(a, t):
-        place = pl.ds(pl.multiple_of(t * 64, 64), 64)
+        place = pl.ds(pl.multiple_of(near_chunk(1 - zl, t) * 64, 64), 64)
         return pltpu.make_async_remote_copy(
             src_ref=twin_out.at[a, place],
             dst_ref=twin_in.at[a, place],
@@ -275,12 +335,14 @@
                 device_id_type=MESH,
             ).wait_recv()
 
-    tok[...] = jnp.zeros_like(tok)
+    swap[...] = one_hot(SLOTS, SLOTS, swap_slots)
+    tok[TOKENS - 4 :, :] = jnp.zeros((PAD - TOKENS + 4, WIDTH), BF16)
+    go[TOKENS - 4 :, :] = jnp.zeros((PAD - TOKENS + 4, WIDTH), BF16)
+    for copy in i_copies:
+        copy.wait()
     tok[0:TOKENS, :] = tok_ref[0]
-    go[...] = jnp.zeros_like(go)
     go[0:TOKENS, :] = go_ref[0]
-    swap = one_hot(SLOTS, SLOTS, swap_slots)
-    spp[...] = dot(sp_ref[...], swap).astype(BF16)
+    spp[...] = dot(sp_ref[...], swap[...]).astype(BF16)
     logits = dot(tok[...], spp[...])
     valid = lax.broadcasted_iota(jnp.int32, (PAD, SLOTS), 0) < TOKENS
     masked = jnp.where(valid, logits, -1e30)
@@ -288,75 +350,78 @@
     dispatch = raised / jnp.sum(raised, axis=0, keepdims=True)
     disp[...] = dispatch
     disp_b[...] = dispatch.astype(BF16)
-    plane_out[0] = dot(disp_b[...], tok[...], 0, 0).astype(BF16)
+    plane_out[0, :, 0:HALF] = dot(disp_b[...], tok[:, 0:HALF], 0, 0).astype(BF16)
     pl.semaphore_wait(barrier, 30)
-    plane_start(0)
+    half_start(0)
+    plane_out[0, :, HALF:WIDTH] = dot(disp_b[...], tok[:, HALF:WIDTH], 0, 0).astype(BF16)
+    half_start(1)
     raised = jnp.exp(logits - jnp.max(logits, axis=1, keepdims=True))
     combine = raised / jnp.sum(raised, axis=1, keepdims=True)
     comb[...] = combine
     plane_out[1] = dot(combine.astype(BF16), go[...], 0, 0).astype(BF16)
     plane_start(1)
+    line[...] = one_hot(SLOTS, SLOTS, to_line)
+    for h in range(2):
+        half_finish(h)
+        columns = pl.ds(h * HALF, HALF)
+        line_out[0, :, columns] = dot(line[...], plane_in[0, :, columns]).astype(BF16)
+        line_start(0, columns)
+    plane[...] = one_hot(SLOTS, SLOTS, to_plane)
     tok_t[...] = tok[...].T
-
-    line = one_hot(SLOTS, SLOTS, to_line)
-    for a in range(2):
-        plane_finish(a)
-        line_out[a] = dot(line, plane_in[a]).astype(BF16)
-        line_start(a)
-    pass_on(0)
+    pass_on(0, 1)
+    plane_finish(1)
+    line_out[1] = dot(line[...], plane_in[1]).astype(BF16)
+    line_start(1)
+    pass_on(0, 2)
+    pass_on(0, 3)
+    own_finish(0)
     for copy in w_copies:
         copy.wait()
-    far_finish(0)
-
-    @pl.loop(0, HALF_HIDDEN // TILE)
-    def _(j):
-        tile = pl.ds(pl.multiple_of(j * TILE, TILE), TILE)
-        pre = dot(rows[0], win[:, tile])
-        square = pre * pre
-        tanh = jnp.tanh(ROOT * pre * (1.0 + 0.044715 * square))
-        half = 0.5 * (1.0 + tanh)
-        act[:, tile] = (pre * half).astype(BF16)
-        slope[:, tile] = half + (0.5 * ROOT) * pre * (1.0 - tanh * tanh) * (
-            1.0 + (3 * 0.044715) * square
-        )
-
-    def send_back(a, wide, weight, weight_dim):
-        def piece(place, j):
+
+    def activate(place):
+        @pl.loop(0, HALF_HIDDEN // TILE)
+        def _(j):
+            tile = pl.ds(pl.multiple_of(j * TILE, TILE), TILE)
+            pre = dot(rows[0, place], win[:, tile])
+            square = pre * pre
+            tanh = jnp.tanh(ROOT * pre * (1.0 + 0.044715 * square))
+            half = 0.5 * (1.0 + tanh)
+            act[place, tile] = (pre * half).astype(BF16)
+            slope[place, tile] = half + (0.5 * ROOT) * pre * (1.0 - tanh * tanh) * (
+                1.0 + (3 * 0.044715) * square
+            )
+
+    def twin_rows(wide, weight, weight_dim, place, target, cast):
+        @pl.loop(0, WIDTH // TILE)
+        def _(j):
             tile = pl.ds(pl.multiple_of(j * TILE, TILE), TILE)
             if weight_dim == 0:
-                return tile, dot(wide[place], weight[:, tile])
-            return tile, dot(wide[place], weight[tile, :], 1, 1)
-
-        @pl.loop(0, WIDTH // TILE)
-        def _(j):
-            tile, value = piece(far_rows, j)
-            twin_out[a, :, tile] = value.astype(BF16)
-
-        @pl.loop(0, 4)
-        def _(t):
-            twin_copy(a, t).start()
-
-        @pl.loop(0, WIDTH // TILE)
-        def _(j):
-            tile, value = piece(near_rows, j)
-            own[:, tile] = value
-
-    def sum_back(a):
-        @pl.loop(0, 4)
-        def _(t):
-            twin_copy(a, t).wait_recv()
-
-        line_out[2 + a] = (own[...] + twin_in[a].astype(F32)).astype(BF16)
-
-        @pl.loop(1, 8)
-        def _(j):
-            back_copy(a, j).start()
-
-        line_in[a, block32(zh * 2 + c)] = line_out[2 + a, block32(near_row(0, c) - 8 * zl)]
-
-    send_back(0, act, wout, 0)
-    pass_on(1)
-    sum_back(0)
+                value = dot(wide[place], weight[:, tile])
+            else:
+                value = dot(wide[place], weight[tile, :], 1, 1)
+            target[:, tile] = value.astype(cast)
+
+    def sum_back(a, t):
+        twin_copy(a, t).wait_recv()
+        place = pl.ds(pl.multiple_of(near_chunk(zl, t) * 64, 64), 64)
+        line_out[2 + a, place] = (own[a, place] + twin_in[a, place].astype(F32)).astype(BF16)
+        back_copy(a, 2 * t + 1).start()
+        if t > 0:
+            back_copy(a, 2 * t).start()
+        else:
+            line_in[a, block32(zh * 2 + c)] = line_out[2 + a, block32(near_row(0, c) - 8 * zl)]
+
+    activate(near_rows)
+    pass_on(1, 1)
+    pass_on(1, 2)
+    pass_on(1, 3)
+    own_finish(1)
+    far_finish(0)
+    activate(far_rows)
+    twin_rows(act, wout, 0, far_rows, twin_out.at[0], BF16)
+    for t in (3, 2, 1, 0):
+        twin_copy(0, t).start()
+    twin_rows(act, wout, 0, near_rows, own.at[0], F32)
     far_finish(1)
 
     @pl.loop(0, HALF_HIDDEN // TILE)
@@ -364,12 +429,11 @@
         tile = pl.ds(pl.multiple_of(j * TILE, TILE), TILE)
         gpre[:, tile] = (dot(rows[1], wout[tile, :], 1, 1) * slope[:, tile]).astype(BF16)
 
-    send_back(1, gpre, win, 1)
-    plane = one_hot(SLOTS, SLOTS, to_plane)
-    back_finish(0)
-    plane_out[2] = dot(plane, line_in[0]).astype(BF16)
-    plane_start(2)
-    sum_back(1)
+    twin_rows(gpre, win, 1, far_rows, twin_out.at[1], BF16)
+    for t in (3, 2, 1, 0):
+        sum_back(0, t)
+        twin_copy(1, t).start()
+    twin_rows(gpre, win, 1, near_rows, own.at[1], F32)
 
     def out_copies(j):
         tile = pl.ds(pl.multiple_of(j * TILE, TILE), TILE)
@@ -385,6 +449,24 @@
         gwo[tile, :] = dot(act[:, tile], rows[1], 0, 0).astype(BF16)
         out_copies(j).start()
 
+    sum_back(1, 3)
+    sum_back(1, 2)
+    back_finish(0)
+    plane_out[2] = dot(plane[...], line_in[0]).astype(BF16)
+    plane_start(2)
+    sum_back(1, 1)
+    sum_back(1, 0)
+    plane_finish(2)
+    gc = dot(go[...], plane_in[2], 1, 1)
+    weight = comb[...]
+    part = dot(
+        (weight * (gc - jnp.sum(gc * weight, axis=1, keepdims=True))).astype(BF16), swap[...]
+    ).astype(BF16)
+    acc_t[...] = dot(part, sp_ref[...], 1, 1)
+    grad_half = dot(tok_t[...], part)
+    grad[0] = grad_half[:, 0:128]
+    grad[1] = grad_half[:, 128:256]
+
     @pl.loop(0, WIDTH // TILE)
     def _(j):
         tile = pl.ds(pl.multiple_of(j * TILE, TILE), TILE)
@@ -392,41 +474,33 @@
         in_copies(j).start()
 
     back_finish(1)
-    plane_out[3] = dot(plane, line_in[1]).astype(BF16)
+    plane_out[3] = dot(plane[...], line_in[1]).astype(BF16)
     plane_start(3)
-    plane_finish(2)
-    gc = dot(go[...], plane_in[2], 1, 1)
-    weight = comb[...]
-    part = dot(
-        (weight * (gc - jnp.sum(gc * weight, axis=1, keepdims=True))).astype(BF16), swap
-    ).astype(BF16)
-    acc_t[...] = dot(part, sp_ref[...], 1, 1)
-    grad_half = dot(tok_t[...], part)
-    grad[0] = grad_half[:, 0:128]
-    grad[1] = grad_half[:, 128:256]
     plane_finish(3)
     gd = dot(tok[...], plane_in[3], 1, 1)
     weight = disp[...]
     part = dot(
-        (weight * (gd - jnp.sum(gd * weight, axis=0, keepdims=True))).astype(BF16), swap
+        (weight * (gd - jnp.sum(gd * weight, axis=0, keepdims=True))).astype(BF16), swap[...]
     ).astype(BF16)
-    grad_half = dot(tok_t[...], part)
-    grad[0] += grad_half[:, 0:128]
-    grad[1] += grad_half[:, 128:256]
-
+    part_s[...] = part
+
+    def half(index):
+        return pl.ds(pl.multiple_of(index * 128, 128), 128)
+
+    other = dot(tok_t[...], part_s[:, half(c ^ 1)])
+    core_out[...] = (grad[c ^ 1] + other).astype(BF16)
     core_copy = pltpu.make_async_remote_copy(
-        src_ref=grad.at[c ^ 1],
-        dst_ref=grad_core,
+        src_ref=core_out,
+        dst_ref=core_in,
         send_sem=g_send.at[0],
         recv_sem=g_recv.at[0],
         device_id=sibling,
         device_id_type=MESH,
     )
     core_copy.start()
-    total = acc_t[...] + dot(part, sp_ref[...], 1, 1) + dot(disp_b[...], plane_in[3])
-    gt_ref[0] = total[0:TOKENS]
+    grad[c] += dot(tok_t[...], part_s[:, half(c)])
     core_copy.wait_recv()
-    ar_out[...] = (grad[c] + grad_core[...]).astype(BF16)
+    ar_out[...] = (grad[c] + core_in[...].astype(F32)).astype(BF16)
 
     def block48(index):
         return pl.ds(pl.multiple_of(index * 48, 48), 48)
@@ -447,6 +521,13 @@
         reduce_copy(k).start()
 
     ar_in[block48(mine)] = ar_out[block48(mine)]
+    total = acc_t[...] + dot(part, sp_ref[...], 1, 1) + dot(disp_b[...], plane_in[3])
+    for column in range(WIDTH // 128):
+        gt[pl.ds(column, TOKENS, stride=WIDTH // 128), :] = total[
+            0:TOKENS, 128 * column : 128 * column + 128
+        ]
+    gt_copy = pltpu.make_async_copy(gt, gt_hbm, o_sem.at[0, 6])
+    gt_copy.start()
 
     @pl.loop(1, 16)
     def _(k):
@@ -473,6 +554,31 @@
 
     z_in[z] = z_out[...]
 
+    @pl.loop(1, 16)
+    def _(k):
+        for h in range(2):
+            half_copy(h, k).wait_send()
+        for a in range(1, 4):
+            plane_copy(a, k).wait_send()
+
+    @pl.loop(1, 8)
+    def _(k):
+        for a in range(2):
+            line_copy(a, k).wait_send()
+            back_copy(a, k).wait_send()
+
+    @pl.loop(0, 8)
+    def _(k):
+        for a in range(2):
+            forward(a, k).wait_send()
+
+    @pl.loop(0, 4)
+    def _(t):
+        for a in range(2):
+            twin_copy(a, t).wait_send()
+
+    core_copy.wait_send()
+
     @pl.loop(1, 8)
     def _(k):
         z_copy(k).wait_recv()
@@ -480,7 +586,7 @@
     line_sum = z_in[0].astype(F32)
     for k in range(1, 8):
         line_sum += z_in[k].astype(F32)
-    done[c, block48(mine)] = line_sum
+    done[c, block48(mine)] = line_sum.astype(BF16)
 
     def gather_copy(k):
         px, py = plane_peer(k)
@@ -496,6 +602,24 @@
     @pl.loop(1, 16)
     def _(k):
         gather_copy(k).start()
+
+    @pl.loop(1, 16)
+    def _(k):
+        reduce_copy(k).wait_send()
+
+    @pl.loop(1, 8)
+    def _(k):
+        z_copy(k).wait_send()
+
+    @pl.loop(0, HALF_HIDDEN // TILE)
+    def _(j):
+        out_copies(j).wait()
+
+    @pl.loop(0, WIDTH // TILE)
+    def _(j):
+        in_copies(j).wait()
+
+    gt_copy.wait()
 
     @pl.loop(1, 16)
     def _(k):
@@ -511,50 +635,33 @@
     )
     last_copy.start()
 
+    gsp[:, half(c)] = done[c]
+
     @pl.loop(1, 16)
     def _(k):
-        for a in range(4):
-            plane_copy(a, k).wait_send()
-        reduce_copy(k).wait_send()
         gather_copy(k).wait_send()
 
-    @pl.loop(1, 8)
-    def _(k):
-        z_copy(k).wait_send()
-        for a in range(2):
-            line_copy(a, k).wait_send()
-            back_copy(a, k).wait_send()
-
-    @pl.loop(0, 8)
-    def _(k):
-        for a in range(2):
-            forward(a, k).wait_send()
-
-    @pl.loop(0, 4)
-    def _(t):
-        for a in range(2):
-            twin_copy(a, t).wait_send()
-
-    core_copy.wait_send()
-
-    @pl.loop(0, HALF_HIDDEN // TILE)
-    def _(j):
-        out_copies(j).wait()
-
-    @pl.loop(0, WIDTH // TILE)
-    def _(j):
-        in_copies(j).wait()
-
     last_copy.wait()
-    gsp_ref[:, 0:128] = done[0]
-    gsp_ref[:, 128:256] = done[1]
+    gsp[:, half(c ^ 1)] = done[c ^ 1]
+    gsp_copy = pltpu.make_async_copy(gsp, gsp_hbm, o_sem.at[0, 7])
+    gsp_copy.start()
+    gsp_copy.wait()
 
 
 def body(tokens, grad_out, slot_param, weight_in, weight_out):
-    vmem = pl.BlockSpec(memory_space=pltpu.VMEM)
+    flat = (tokens.shape[1] * tokens.shape[2] // 128, 128)
     hbm = pl.BlockSpec(memory_space=pl.ANY)
     dma = pltpu.SemaphoreType.DMA
     buffers = [
+        (tokens.shape, BF16),
+        (tokens.shape, BF16),
+        (slot_param.shape, BF16),
+        ((SLOTS, SLOTS), BF16),
+        ((SLOTS, SLOTS), BF16),
+        ((SLOTS, SLOTS), BF16),
+        ((PAD, SLOTS), BF16),
+        (flat, F32),
+        (slot_param.shape, BF16),
         ((PAD, WIDTH), BF16),
         ((PAD, WIDTH), BF16),
         ((WIDTH, PAD), BF16),
@@ -571,7 +678,7 @@
         ((2, ROWS, WIDTH), BF16),
         ((2, NEAR, WIDTH), BF16),
         ((2, NEAR, WIDTH), BF16),
-        ((NEAR, WIDTH), F32),
+        ((2, NEAR, WIDTH), F32),
         ((ROWS, HALF_HIDDEN), BF16),
         ((ROWS, HALF_HIDDEN), F32),
         ((ROWS, HALF_HIDDEN), BF16),
@@ -579,29 +686,30 @@
         ((HALF_HIDDEN, WIDTH), BF16),
         ((PAD, WIDTH), F32),
         ((2, WIDTH, 128), F32),
-        ((WIDTH, 128), F32),
+        ((WIDTH, 128), BF16),
+        ((WIDTH, 128), BF16),
         ((WIDTH, 128), BF16),
         ((WIDTH, 128), BF16),
         ((48, 128), BF16),
         ((8, 48, 128), BF16),
-        ((2, WIDTH, 128), F32),
+        ((2, WIDTH, 128), BF16),
     ]
-    return pl.pallas_call(
+    grad_tokens, grad_in, grad_out, grad_slots = pl.pallas_call(
         kernel,
         out_shape=(
-            jax.ShapeDtypeStruct(tokens.shape, F32),
+            jax.ShapeDtypeStruct(flat, F32),
             jax.ShapeDtypeStruct(weight_in.shape, BF16),
             jax.ShapeDtypeStruct(weight_out.shape, BF16),
-            jax.ShapeDtypeStruct(slot_param.shape, F32),
+            jax.ShapeDtypeStruct(slot_param.shape, BF16),
         ),
-        in_specs=[vmem, vmem, vmem, hbm, hbm],
-        out_specs=(vmem, hbm, hbm, vmem),
+        in_specs=[pl.BlockSpec(memory_space=pltpu.HBM)] * 5,
+        out_specs=(hbm,) * 4,
         scratch_shapes=[pltpu.VMEM(shape, kind) for shape, kind in buffers]
         + [
-            dma((2,)),
+            dma((5,)),
             dma((2, 8)),
-            dma((4, 16)),
-            dma((4, 16)),
+            dma((5, 16)),
+            dma((5, 16)),
             dma((4, 8)),
             dma((4, 8)),
             dma((2, 8)),
@@ -616,9 +724,10 @@
             dma((8,)),
         ],
         compiler_params=pltpu.CompilerParams(
-            collective_id=0, has_side_effects=True, vmem_limit_bytes=56 * 1024 * 1024
+            collective_id=0, has_side_effects=True, vmem_limit_bytes=46 * 1024 * 1024
         ),
     )(tokens, grad_out, slot_param, weight_in, weight_out)
+    return grad_tokens.reshape(tokens.shape), grad_in, grad_out, grad_slots.astype(F32)
 
 
 def solution(mesh):

time: 137 us -> 114 us (0.83)
  Pallas kernels: 127 us -> 106 us
  local copies, waits for them, and re-layouts: 8.44 us -> 6.55 us
    pallas_call x1, Pallas kernels: 127 us -> 106 us  [body(): pl.pallas_call(kernel, out_shape=(jax.ShapeDtypeStruct(flat, F32), jax.Sh...]
    pallas_call x1 -> x0, local copies, waits for them, and re-layouts: 2.51 us -> none  [body(): pl.pallas_call(kernel, out_shape=(jax.ShapeDtypeStruct(tokens.shape, F32)...]
    unnamed x7 -> x9, local copies, waits for them, and re-layouts: 5.93 us -> 6.55 us
where the time goes in v2:
time: 114 us
  Pallas kernels  106 us (93%)
  local copies, waits for them, and re-layouts  6.55 us (6%)
    pallas_call x1, Pallas kernels, body(): pl.pallas_call(kernel, out_shape=(jax.ShapeDtypeStruct(flat, F32), jax.Sh...  106 us
    unnamed x9, local copies, waits for them, and re-layouts  6.55 us

profile of v2, /device:TPU:1, one launch (start us, length us, event | category | flops | bytes accessed | tf_op | source)
XLA Modules:
  0.0 113.8 jit_solution(3913851472270360026)
XLA Ops:
  0.6 0.0 copy-start
  0.6 1.0 copy-done
  1.6 0.0 copy-start.1
  1.6 1.0 copy-done.1
  2.6 0.0 copy-start.2
  2.6 1.0 copy-done.2
  3.6 105.6 %shard_map.84 = (f32[1176,128]{1,0:T(8,128)S(1)}, bf16[1,768,1536]{2,1,0:T(8,128)(2,1)S(1)}, bf16[1,1536,768]{2,1,0:T(8,128)(2,1)S(1)}, bf16[768,256]{1,0:T(8,128)(2,1)S(1)}) custom-call(bf16[1,196,768]{2,1,0:T(8,128)(2,1)S(1)} %copy-done.1, bf16[1,196,768]{2,1,0:T(8,128)(2,1)S(1)} %copy-done.2, bf16[768,256]{1,0:T(8,128)(2,1)S(1)} %copy-done, ...), custom_call_target="tpu_custom_call" | custom-call | tf_op jit(solution)/shard_map/pallas_call | solution.py:697
  109.2 0.9 convert_element_type.3
  110.1 0.8 copy.14
  111.0 1.4 %copy.15 = bf16[1,768,1536]{2,1,0:T(8,128)(2,1)} copy(bf16[1,768,1536]{2,1,0:T(8,128)(2,1)S(1)} %get-tuple-element.25) | data formatting | bytes 4718592
  112.4 1.4 %copy.16 = bf16[1,1536,768]{2,1,0:T(8,128)(2,1)} copy(bf16[1,1536,768]{2,1,0:T(8,128)(2,1)S(1)} %get-tuple-element.26) | data formatting | bytes 4718592
Async XLA Ops:
  0.6 1.0 copy-start
  1.6 1.0 copy-start.1
  2.6 1.0 copy-start.2

commit v3 on v2

--- a/solution.py
+++ b/solution.py
@@ -443,12 +443,6 @@
         tile = pl.ds(pl.multiple_of(j * TILE, TILE), TILE)
         return pltpu.make_async_copy(gwi.at[tile], gwi_hbm.at[0, tile], o_sem.at[1, j])
 
-    @pl.loop(0, HALF_HIDDEN // TILE)
-    def _(j):
-        tile = pl.ds(pl.multiple_of(j * TILE, TILE), TILE)
-        gwo[tile, :] = dot(act[:, tile], rows[1], 0, 0).astype(BF16)
-        out_copies(j).start()
-
     sum_back(1, 3)
     sum_back(1, 2)
     back_finish(0)
@@ -467,15 +461,22 @@
     grad[0] = grad_half[:, 0:128]
     grad[1] = grad_half[:, 128:256]
 
+    back_finish(1)
+    plane_out[3] = dot(plane[...], line_in[1]).astype(BF16)
+    plane_start(3)
+
+    @pl.loop(0, HALF_HIDDEN // TILE)
+    def _(j):
+        tile = pl.ds(pl.multiple_of(j * TILE, TILE), TILE)
+        gwo[tile, :] = dot(act[:, tile], rows[1], 0, 0).astype(BF16)
+        out_copies(j).start()
+
     @pl.loop(0, WIDTH // TILE)
     def _(j):
         tile = pl.ds(pl.multiple_of(j * TILE, TILE), TILE)
         gwi[tile, :] = dot(rows[0, :, tile], gpre[...], 0, 0).astype(BF16)
         in_copies(j).start()
 
-    back_finish(1)
-    plane_out[3] = dot(plane[...], line_in[1]).astype(BF16)
-    plane_start(3)
     plane_finish(3)
     gd = dot(tok[...], plane_in[3], 1, 1)
     weight = disp[...]
@@ -649,6 +650,7 @@
 
 
 def body(tokens, grad_out, slot_param, weight_in, weight_out):
+    arrays = (tokens, grad_out, slot_param, weight_in, weight_out)
     flat = (tokens.shape[1] * tokens.shape[2] // 128, 128)
     hbm = pl.BlockSpec(memory_space=pl.ANY)
     dma = pltpu.SemaphoreType.DMA
@@ -726,7 +728,7 @@
         compiler_params=pltpu.CompilerParams(
             collective_id=0, has_side_effects=True, vmem_limit_bytes=46 * 1024 * 1024
         ),
-    )(tokens, grad_out, slot_param, weight_in, weight_out)
+    )(*(pltpu.with_memory_space_constraint(array, pltpu.HBM) for array in arrays))
     return grad_tokens.reshape(tokens.shape), grad_in, grad_out, grad_slots.astype(F32)
 
 

time: 114 us -> 110 us (0.965)
  local copies, waits for them, and re-layouts: 6.55 us -> 3.63 us
  Pallas kernels: 106 us -> 104 us
    unnamed x9 -> x3, local copies, waits for them, and re-layouts: 6.55 us -> 3.63 us
    pallas_call x1, Pallas kernels: 106 us -> 104 us  [body(): pl.pallas_call(kernel, out_shape=(jax.ShapeDtypeStruct(flat, F32), jax.Sh...]
where the time goes in v3:
time: 110 us
  Pallas kernels  104 us (95%)
  local copies, waits for them, and re-layouts  3.63 us (3%)
    pallas_call x1, Pallas kernels, body(): pl.pallas_call(kernel, out_shape=(jax.ShapeDtypeStruct(flat, F32), jax.Sh...  104 us
    unnamed x3, local copies, waits for them, and re-layouts  3.63 us

profile of v3, /device:TPU:1, one launch (start us, length us, event | category | flops | bytes accessed | tf_op | source)
XLA Modules:
  0.0 109.7 jit_solution(12731018844316452364)
XLA Ops:
  0.6 104.5 %shard_map.84 = (f32[1176,128]{1,0:T(8,128)S(1)}, bf16[1,768,1536]{2,1,0:T(8,128)(2,1)S(1)}, bf16[1,1536,768]{2,1,0:T(8,128)(2,1)S(1)}, bf16[768,256]{1,0:T(8,128)(2,1)S(1)}) custom-call(bf16[1,196,768]{2,1,0:T(8,128)(2,1)} %tok_hbm.1, bf16[1,196,768]{2,1,0:T(8,128)(2,1)} %go_hbm.1, bf16[768,256]{1,0:T(8,128)(2,1)} %sp_hbm.1, bf16[1,768,1536]{2,1,0:T(8,128)(2,1)} %win_hbm.1, ...), custom_call_target="tpu_custom_call" | custom-call | tf_op jit(solution)/shard_map/pallas_call | solution.py:699
  105.1 0.9 convert_element_type.3
  106.1 0.8 copy.14
  106.9 1.4 %copy.15 = bf16[1,768,1536]{2,1,0:T(8,128)(2,1)} copy(bf16[1,768,1536]{2,1,0:T(8,128)(2,1)S(1)} %get-tuple-element.25) | data formatting | bytes 4718592
  108.3 1.4 %copy.16 = bf16[1,1536,768]{2,1,0:T(8,128)(2,1)} copy(bf16[1,1536,768]{2,1,0:T(8,128)(2,1)S(1)} %get-tuple-element.26) | data formatting | bytes 4718592

commit v4 on v3

--- a/solution.py
+++ b/solution.py
@@ -66,7 +66,6 @@
     swap,
     part_s,
     gt,
-    gsp,
     tok,
     go,
     tok_t,
@@ -114,6 +113,7 @@
     g_recv,
     z_send,
     z_recv,
+    g_result,
 ):
     expert = lax.axis_index("expert")
     zl = lax.axis_index("hid")
@@ -338,11 +338,10 @@
     swap[...] = one_hot(SLOTS, SLOTS, swap_slots)
     tok[TOKENS - 4 :, :] = jnp.zeros((PAD - TOKENS + 4, WIDTH), BF16)
     go[TOKENS - 4 :, :] = jnp.zeros((PAD - TOKENS + 4, WIDTH), BF16)
-    for copy in i_copies:
-        copy.wait()
+    i_copies[0].wait()
+    spp[...] = dot(sp_ref[...], swap[...]).astype(BF16)
+    i_copies[1].wait()
     tok[0:TOKENS, :] = tok_ref[0]
-    go[0:TOKENS, :] = go_ref[0]
-    spp[...] = dot(sp_ref[...], swap[...]).astype(BF16)
     logits = dot(tok[...], spp[...])
     valid = lax.broadcasted_iota(jnp.int32, (PAD, SLOTS), 0) < TOKENS
     masked = jnp.where(valid, logits, -1e30)
@@ -355,6 +354,8 @@
     half_start(0)
     plane_out[0, :, HALF:WIDTH] = dot(disp_b[...], tok[:, HALF:WIDTH], 0, 0).astype(BF16)
     half_start(1)
+    i_copies[2].wait()
+    go[0:TOKENS, :] = go_ref[0]
     raised = jnp.exp(logits - jnp.max(logits, axis=1, keepdims=True))
     combine = raised / jnp.sum(raised, axis=1, keepdims=True)
     comb[...] = combine
@@ -411,8 +412,8 @@
         else:
             line_in[a, block32(zh * 2 + c)] = line_out[2 + a, block32(near_row(0, c) - 8 * zl)]
 
+    pass_on(1, 1)
     activate(near_rows)
-    pass_on(1, 1)
     pass_on(1, 2)
     pass_on(1, 3)
     own_finish(1)
@@ -422,18 +423,23 @@
     for t in (3, 2, 1, 0):
         twin_copy(0, t).start()
     twin_rows(act, wout, 0, near_rows, own.at[0], F32)
+
+    def pull(place):
+        @pl.loop(0, HALF_HIDDEN // TILE)
+        def _(j):
+            tile = pl.ds(pl.multiple_of(j * TILE, TILE), TILE)
+            gpre[place, tile] = (dot(rows[1, place], wout[tile, :], 1, 1) * slope[place, tile]).astype(
+                BF16
+            )
+
+    pull(near_rows)
+    twin_rows(gpre, win, 1, near_rows, own.at[1], F32)
     far_finish(1)
-
-    @pl.loop(0, HALF_HIDDEN // TILE)
-    def _(j):
-        tile = pl.ds(pl.multiple_of(j * TILE, TILE), TILE)
-        gpre[:, tile] = (dot(rows[1], wout[tile, :], 1, 1) * slope[:, tile]).astype(BF16)
-
+    pull(far_rows)
     twin_rows(gpre, win, 1, far_rows, twin_out.at[1], BF16)
     for t in (3, 2, 1, 0):
         sum_back(0, t)
         twin_copy(1, t).start()
-    twin_rows(gpre, win, 1, near_rows, own.at[1], F32)
 
     def out_copies(j):
         tile = pl.ds(pl.multiple_of(j * TILE, TILE), TILE)
@@ -453,10 +459,8 @@
     plane_finish(2)
     gc = dot(go[...], plane_in[2], 1, 1)
     weight = comb[...]
-    part = dot(
-        (weight * (gc - jnp.sum(gc * weight, axis=1, keepdims=True))).astype(BF16), swap[...]
-    ).astype(BF16)
-    acc_t[...] = dot(part, sp_ref[...], 1, 1)
+    part = (weight * (gc - jnp.sum(gc * weight, axis=1, keepdims=True))).astype(BF16)
+    acc_t[...] = dot(part, spp[...], 1, 1)
     grad_half = dot(tok_t[...], part)
     grad[0] = grad_half[:, 0:128]
     grad[1] = grad_half[:, 128:256]
@@ -480,9 +484,7 @@
     plane_finish(3)
     gd = dot(tok[...], plane_in[3], 1, 1)
     weight = disp[...]
-    part = dot(
-        (weight * (gd - jnp.sum(gd * weight, axis=0, keepdims=True))).astype(BF16), swap[...]
-    ).astype(BF16)
+    part = (weight * (gd - jnp.sum(gd * weight, axis=0, keepdims=True))).astype(BF16)
     part_s[...] = part
 
     def half(index):
@@ -522,7 +524,7 @@
         reduce_copy(k).start()
 
     ar_in[block48(mine)] = ar_out[block48(mine)]
-    total = acc_t[...] + dot(part, sp_ref[...], 1, 1) + dot(disp_b[...], plane_in[3])
+    total = acc_t[...] + dot(part, spp[...], 1, 1) + dot(disp_b[...], plane_in[3])
     for column in range(WIDTH // 128):
         gt[pl.ds(column, TOKENS, stride=WIDTH // 128), :] = total[
             0:TOKENS, 128 * column : 128 * column + 128
@@ -587,7 +589,7 @@
     line_sum = z_in[0].astype(F32)
     for k in range(1, 8):
         line_sum += z_in[k].astype(F32)
-    done[c, block48(mine)] = line_sum.astype(BF16)
+    done[c, block48(mine)] = dot(line_sum.astype(BF16), swap[0:128, 0:128]).astype(BF16)
 
     def gather_copy(k):
         px, py = plane_peer(k)
@@ -636,17 +638,38 @@
     )
     last_copy.start()
 
-    gsp[:, half(c)] = done[c]
+    def result_copy(index, slot):
+        return pltpu.make_async_copy(done.at[index], gsp_hbm.at[:, half(index)], g_result.at[slot])
+
+    result_copy(c, 0).start()
 
     @pl.loop(1, 16)
     def _(k):
         gather_copy(k).wait_send()
 
     last_copy.wait()
-    gsp[:, half(c ^ 1)] = done[c ^ 1]
-    gsp_copy = pltpu.make_async_copy(gsp, gsp_hbm, o_sem.at[0, 7])
-    gsp_copy.start()
-    gsp_copy.wait()
+    result_copy(c ^ 1, 1).start()
+    result_copy(c, 0).wait()
+    result_copy(c ^ 1, 1).wait()
+
+
+def finish(gt_in, gwi_in, gwo_in, gsp_in, gt_out, gwi_out, gwo_out, gsp_out, narrow, wide, sem):
+    fetch = pltpu.make_async_copy(gsp_in, narrow, sem.at[0])
+    fetch.start()
+    copies = [
+        pltpu.make_async_copy(gwi_in, gwi_out, sem.at[1]),
+        pltpu.make_async_copy(gwo_in, gwo_out, sem.at[2]),
+        pltpu.make_async_copy(gt_in, gt_out, sem.at[3]),
+    ]
+    for copy in copies:
+        copy.start()
+    fetch.wait()
+    wide[...] = narrow[...].astype(F32)
+    last = pltpu.make_async_copy(wide, gsp_out, sem.at[4])
+    last.start()
+    for copy in copies:
+        copy.wait()
+    last.wait()
 
 
 def body(tokens, grad_out, slot_param, weight_in, weight_out):
@@ -663,7 +686,6 @@
         ((SLOTS, SLOTS), BF16),
         ((PAD, SLOTS), BF16),
         (flat, F32),
-        (slot_param.shape, BF16),
         ((PAD, WIDTH), BF16),
         ((PAD, WIDTH), BF16),
         ((WIDTH, PAD), BF16),
@@ -724,12 +746,30 @@
             dma((2,)),
             dma((8,)),
             dma((8,)),
+            dma((2,)),
         ],
         compiler_params=pltpu.CompilerParams(
             collective_id=0, has_side_effects=True, vmem_limit_bytes=46 * 1024 * 1024
         ),
     )(*(pltpu.with_memory_space_constraint(array, pltpu.HBM) for array in arrays))
-    return grad_tokens.reshape(tokens.shape), grad_in, grad_out, grad_slots.astype(F32)
+    grad_tokens, grad_in, grad_out, grad_slots = pl.pallas_call(
+        finish,
+        out_shape=(
+            jax.ShapeDtypeStruct(flat, F32),
+            jax.ShapeDtypeStruct(weight_in.shape, BF16),
+            jax.ShapeDtypeStruct(weight_out.shape, BF16),
+            jax.ShapeDtypeStruct(slot_param.shape, F32),
+        ),
+        in_specs=[hbm] * 4,
+        out_specs=(hbm,) * 4,
+        scratch_shapes=[
+            pltpu.VMEM(slot_param.shape, BF16),
+            pltpu.VMEM(slot_param.shape, F32),
+            dma((5,)),
+        ],
+        compiler_params=pltpu.CompilerParams(vmem_limit_bytes=8 * 1024 * 1024),
+    )(grad_tokens, grad_in, grad_out, grad_slots)
+    return grad_tokens.reshape(tokens.shape), grad_in, grad_out, grad_slots
 
 
 def solution(mesh):

time: 110 us -> 108 us (0.982)
  local copies, waits for them, and re-layouts: 3.63 us -> 0 us
  Pallas kernels: 104 us -> 107 us
    unnamed x3 -> x0, local copies, waits for them, and re-layouts: 3.63 us -> none
    pallas_call x0 -> x1, Pallas kernels: none -> 2.84 us  [body(): pl.pallas_call(finish, out_shape=(jax.ShapeDtypeStruct(flat, F32), jax.Sh...]
where the time goes in v4:
time: 108 us
  Pallas kernels  107 us (99%)
    pallas_call x1, Pallas kernels, body(): pl.pallas_call(kernel, out_shape=(jax.ShapeDtypeStruct(flat, F32), jax.Sh...  104 us
    pallas_call x1, Pallas kernels, body(): pl.pallas_call(finish, out_shape=(jax.ShapeDtypeStruct(flat, F32), jax.Sh...  2.84 us

profile of v4, /device:TPU:1, one launch (start us, length us, event | category | flops | bytes accessed | tf_op | source)
XLA Modules:
  0.0 107.8 jit_solution(18225326637588792623)
XLA Ops:
  0.6 104.3 %shard_map.84 = (f32[1176,128]{1,0:T(8,128)S(1)}, bf16[1,768,1536]{2,1,0:T(8,128)(2,1)S(1)}, bf16[1,1536,768]{2,1,0:T(8,128)(2,1)S(1)}, bf16[768,256]{1,0:T(8,128)(2,1)S(1)}) custom-call(bf16[1,196,768]{2,1,0:T(8,128)(2,1)} %tok_hbm.1, bf16[1,196,768]{2,1,0:T(8,128)(2,1)} %go_hbm.1, bf16[768,256]{1,0:T(8,128)(2,1)} %sp_hbm.1, bf16[1,768,1536]{2,1,0:T(8,128)(2,1)} %win_hbm.1, ...), custom_call_target="tpu_custom_call" | custom-call | tf_op jit(solution)/shard_map/pallas_call | solution.py:721
  104.9 2.8 %shard_map.85 = (f32[1176,128]{1,0:T(8,128)}, bf16[1,768,1536]{2,1,0:T(8,128)(2,1)}, bf16[1,1536,768]{2,1,0:T(8,128)(2,1)}, f32[768,256]{1,0:T(8,128)}) custom-call(f32[1176,128]{1,0:T(8,128)S(1)} %get-tuple-element.12.gt_in, bf16[1,768,1536]{2,1,0:T(8,128)(2,1)S(1)} %get-tuple-element.13.gwi_in, bf16[1,1536,768]{2,1,0:T(8,128)(2,1)S(1)} %get-tuple-element.14.gwo_in, ...), custom_call_target="tpu_custom_call" | custom-call | tf_op jit(solution)/shard_map/pallas_call | solution.py:755

commit v5 on v4

--- a/solution.py
+++ b/solution.py
@@ -192,7 +192,7 @@
         )
 
     def half_start(h):
-        @pl.loop(1, 16)
+        @pl.loop(1, 16, unroll=5)
         def _(k):
             half_copy(h, k).start()
 
@@ -205,7 +205,7 @@
             half_copy(h, k).wait_recv()
 
     def plane_start(a):
-        @pl.loop(1, 16)
+        @pl.loop(1, 16, unroll=5)
         def _(k):
             plane_copy(a, k).start()
 
@@ -519,7 +519,7 @@
             device_id_type=MESH,
         )
 
-    @pl.loop(1, 16)
+    @pl.loop(1, 16, unroll=5)
     def _(k):
         reduce_copy(k).start()
 
@@ -532,7 +532,7 @@
     gt_copy = pltpu.make_async_copy(gt, gt_hbm, o_sem.at[0, 6])
     gt_copy.start()
 
-    @pl.loop(1, 16)
+    @pl.loop(1, 16, unroll=5)
     def _(k):
         reduce_copy(k).wait_recv()
 
@@ -602,7 +602,7 @@
             device_id_type=MESH,
         )
 
-    @pl.loop(1, 16)
+    @pl.loop(1, 16, unroll=5)
     def _(k):
         gather_copy(k).start()
 
@@ -624,7 +624,7 @@
 
     gt_copy.wait()
 
-    @pl.loop(1, 16)
+    @pl.loop(1, 16, unroll=5)
     def _(k):
         gather_copy(k).wait_recv()
 

time: 108 us -> 108 us (level)
  no operation moved by 1% of the time
where the time goes in v5:
time: 108 us
  Pallas kernels  107 us (99%)
    pallas_call x1, Pallas kernels, body(): pl.pallas_call(kernel, out_shape=(jax.ShapeDtypeStruct(flat, F32), jax.Sh...  104 us
    pallas_call x1, Pallas kernels, body(): pl.pallas_call(finish, out_shape=(jax.ShapeDtypeStruct(flat, F32), jax.Sh...  2.84 us

profile of v5, /device:TPU:1, one launch (start us, length us, event | category | flops | bytes accessed | tf_op | source)
XLA Modules:
  0.0 107.7 jit_solution(652636159595995451)
XLA Ops:
  0.6 104.2 %shard_map.84 = (f32[1176,128]{1,0:T(8,128)S(1)}, bf16[1,768,1536]{2,1,0:T(8,128)(2,1)S(1)}, bf16[1,1536,768]{2,1,0:T(8,128)(2,1)S(1)}, bf16[768,256]{1,0:T(8,128)(2,1)S(1)}) custom-call(bf16[1,196,768]{2,1,0:T(8,128)(2,1)} %tok_hbm.1, bf16[1,196,768]{2,1,0:T(8,128)(2,1)} %go_hbm.1, bf16[768,256]{1,0:T(8,128)(2,1)} %sp_hbm.1, bf16[1,768,1536]{2,1,0:T(8,128)(2,1)} %win_hbm.1, ...), custom_call_target="tpu_custom_call" | custom-call | tf_op jit(solution)/shard_map/pallas_call | solution.py:721
  104.8 2.8 %shard_map.85 = (f32[1176,128]{1,0:T(8,128)}, bf16[1,768,1536]{2,1,0:T(8,128)(2,1)}, bf16[1,1536,768]{2,1,0:T(8,128)(2,1)}, f32[768,256]{1,0:T(8,128)}) custom-call(f32[1176,128]{1,0:T(8,128)S(1)} %get-tuple-element.12.gt_in, bf16[1,768,1536]{2,1,0:T(8,128)(2,1)S(1)} %get-tuple-element.13.gwi_in, bf16[1,1536,768]{2,1,0:T(8,128)(2,1)S(1)} %get-tuple-element.14.gwo_in, ...), custom_call_target="tpu_custom_call" | custom-call | tf_op jit(solution)/shard_map/pallas_call | solution.py:755
